TPU v7x, 256 devices: a whole 4x4x8 slice. The times are simulated.
256 devices in a mesh: row: 32 (over z, x), col: 8 (over y, core).
Axes of the slice: x: 4, y: 4, z: 8, core: 2. Of those that a mesh axis runs over, the one named last changes fastest.
Arguments:
- image: bfloat16 [512, 1024, 256], P('row', 'col'), may hold values from -6 to 6
- kernel_one: bfloat16 [3, 3, 256, 256], replicated, may hold values from -0.125 to 0.125
- kernel_two: bfloat16 [3, 3, 256, 512], replicated, may hold values from -0.125 to 0.125
- cotangent: bfloat16 [256, 512, 512], P('row', 'col'), may hold values from -6 to 6
Outputs:
- image_grad: bfloat16 [512, 1024, 256], P('row', 'col')
- update_one: bfloat16 [3, 3, 256, 256], replicated
- update_two: bfloat16 [3, 3, 256, 512], replicated
All inputs are finite; a program needn't handle non-finite values.
Results may differ from a plain program's by a relative error of at most 0.006.
Values may be sent and summed in bfloat16 or wider, within the bound.
A program may use at most 128 MiB of HBM per device.

v0:
```python
import jax
import jax.numpy as jnp
from jax import lax
from jax.sharding import PartitionSpec as P


def padded(shard, sides, width):
    for axis, dim in sides:
        size, length = (lax.axis_size(axis), shard.shape[dim])
        up = [(i, (i + 1) % size) for i in range(size - 1)]
        down = [(j, i) for i, j in up]
        last = lax.slice_in_dim(shard, length - width, length, axis=dim)
        initial = lax.slice_in_dim(shard, 0, width, axis=dim)
        before = lax.ppermute(last, axis, up)
        after = lax.ppermute(initial, axis, down)
        shard = jnp.concatenate([before, shard, after], axis=dim)
    return shard


def passed_along(shard, axis, by):
    size = lax.axis_size(axis)
    pairs = [(i, i + by) for i in range(size) if 0 <= i + by < size]
    return lax.ppermute(shard, axis, pairs)


def conv_local(source, kernel, padding, dilation, layout):
    result = lax.conv_general_dilated(
        source[None],
        kernel,
        (1, 1),
        padding,
        lhs_dilation=dilation,
        dimension_numbers=("NHWC", layout, "NHWC"),
        preferred_element_type=jnp.float32,
    )
    return result[0]


def on_device(image, kernel_one, kernel_two, cotangent):
    rows_here = image.shape[0]
    cols_here = image.shape[1]
    image_pad = padded(image, (("row", 0), ("col", 1)), 1)
    pre_act = conv_local(image_pad, kernel_one, "VALID", (1, 1), "HWIO")
    activ = jax.nn.silu(pre_act).astype(jnp.bfloat16)
    left_edge = passed_along(activ[:, -1:], "col", 1)
    act_cols = jnp.concatenate([left_edge, activ], 1)
    top_edge = passed_along(act_cols[-1:], "row", 1)
    act_pad = jnp.concatenate([top_edge, act_cols], 0)
    rows_two = []
    for row_off in range(3):
        cols_two = []
        for col_off in range(3):
            patch = act_pad[
                row_off : row_off + rows_here - 1 : 2, col_off : col_off + cols_here - 1 : 2
            ]
            cols_two.append(
                jnp.einsum("ijc,ije->ce", patch, cotangent, preferred_element_type=jnp.float32)
            )
        rows_two.append(jnp.stack(cols_two))
    grad_two = jnp.stack(rows_two)
    flipped_two = kernel_two[::-1, ::-1]
    act_full = conv_local(cotangent, flipped_two, ((2, 2), (2, 2)), (2, 2), "HWOI")
    from_right = passed_along(act_full[:, :1], "col", -1)
    act_trim = act_full[:, 1:]
    act_trim = jnp.concatenate([act_trim[:, :-1], act_trim[:, -1:] + from_right], 1)
    from_below = passed_along(act_trim[:1].astype(jnp.bfloat16), "row", -1).astype(jnp.float32)
    act_grad = act_trim[1:]
    act_grad = jnp.concatenate([act_grad[:-1], act_grad[-1:] + from_below], 0)
    sig = jax.nn.sigmoid(pre_act)
    pre_grad = (act_grad * sig * (1.0 + pre_act * (1.0 - sig))).astype(jnp.bfloat16)
    rows_one = []
    for row_off in range(3):
        cols_one = []
        for col_off in range(3):
            patch = image_pad[row_off : row_off + rows_here, col_off : col_off + cols_here]
            cols_one.append(
                jnp.einsum("ijc,ijd->cd", patch, pre_grad, preferred_element_type=jnp.float32)
            )
        rows_one.append(jnp.stack(cols_one))
    grad_one = jnp.stack(rows_one)
    grad_pad = padded(pre_grad, (("row", 0), ("col", 1)), 1)
    image_grad = conv_local(grad_pad, kernel_one[::-1, ::-1], "VALID", (1, 1), "HWOI").astype(
        jnp.bfloat16
    )
    flat_one = grad_one.reshape(-1)
    flat_two = grad_two.reshape(-1)
    total_one, total_two = lax.psum((flat_one, flat_two), ("row", "col"))
    update_one = (total_one * lax.rsqrt(jnp.mean(total_one * total_one) + 1e-06)).astype(
        jnp.bfloat16
    )
    update_two = (total_two * lax.rsqrt(jnp.mean(total_two * total_two) + 1e-06)).astype(
        jnp.bfloat16
    )
    return (image_grad, update_one.reshape(kernel_one.shape), update_two.reshape(kernel_two.shape))


def solution(mesh):
    placed = (P("row", "col", None), P(), P(), P("row", "col", None))
    return jax.shard_map(
        on_device,
        mesh=mesh,
        in_specs=placed,
        out_specs=(P("row", "col", None), P(), P()),
        check_vma=False,
    )
```

profile of v0, /device:TPU:2, one launch (start us, length us, event | category | flops | bytes accessed | tf_op | source)
XLA Modules:
  0.0 440.2 jit_solution(7343728317577428346)
XLA Ops:
  7.2 1.5 copy.73
  9.0 1.7 convolution_select_fusion
  10.7 2.6 copy.37
  13.3 4.1 reshape.29
  17.4 1.9 slice_bitcast_fusion
  19.4 1.4 copy-done.4
  20.8 1.3 collective-permute-start
  22.8 3.4 collective-permute-start.2
  26.2 2.4 collective-permute-start.3
  28.6 1.9 slice.155
  31.5 1.5 fusion.4
  33.2 1.9 fusion.54
  35.0 1.8 copy.41
  36.8 2.5 collective-permute-start.4
  39.3 1.8 copy.42
  41.1 1.3 collective-permute-start.5
  43.1 1.9 collective-permute-start.1
  45.0 1.5 copy.43
  46.5 1.5 copy.44
  47.9 4.4 maximum_bitcast_fusion
  52.3 3.9 copy.64
  56.2 2.5 pad.2.clone
  58.6 3.2 reshape.32
  61.9 1.9 copy.47
  63.8 3.0 convolution_select_fusion.1
  66.9 3.6 maximum_maximum_fusion
  71.4 1.5 copy-done.5
  72.9 1.8 multiply_convert_fusion.2
  74.7 2.7 slice.143
  77.4 2.7 slice.142
  80.1 2.7 slice.146
  82.8 2.7 slice.145
  85.5 1.8 convolution_bitcast_fusion.15
  91.0 4.4 %collective-permute-start.10 = (bf16[16,1,256]{2,1,0:T(2,128)(2,1)S(1)}, bf16[16,1,256]{2,1,0:T(2,128)(2,1)S(1)}, u32[]{:S(2)}, u32[]{:S(2)}) collective-permute-start(bf16[16,1,256]{2,1,0:T(2,128)(2,1)S(1)} %slice.178), channel_id=1, source_target_pairs={{0,1},{1,2},{2,3},{3,4},{4,5},{5,6},{6,7},{8,9},{9,10},{10,11},{11... | collective-permute-start | bytes 24584 | tf_op jit(solution)/shard_map/ppermute | solution.py:23
  95.5 1.1 convolution_bitcast_fusion.3
  96.6 1.1 convolution_bitcast_fusion.4
  101.3 2.6 copy.65
  104.3 2.7 slice.141
  107.5 3.8 collective-permute-start.11
  111.3 2.3 convolution_bitcast_fusion.5
  113.9 1.3 maximum_bitcast_fusion.3
  115.7 2.7 slice.140
  118.4 2.7 slice.139
  121.5 1.5 convolution_bitcast_fusion.6
  123.1 1.4 convolution_bitcast_fusion.7
  124.5 1.4 convolution_bitcast_fusion.8
  127.9 3.4 copy.66
  131.3 4.7 %collective-permute-start.6 = (bf16[1,128,256]{2,1,0:T(8,128)(2,1)S(1)}, bf16[1,128,256]{2,1,0:T(8,128)(2,1)S(1)}, u32[]{:S(2)}, u32[]{:S(2)}) collective-permute-start(bf16[1,128,256]{2,1,0:T(8,128)(2,1)S(1)} %get-tuple-element.19), channel_id=1, source_target_pairs={{0,8},{8,16},{16,24},{24,32},{32,40},{40,48},{48,56},{56,64},{64,7... | collective-permute-start | bytes 196616 | tf_op jit(solution)/shard_map/ppermute | solution.py:14
  135.9 1.9 collective-permute-start.7
  138.0 5.9 %collective-permute-done.7 = bf16[1,128,256]{2,1,0:T(8,128)(2,1)S(1)} collective-permute-done((bf16[1,128,256]{2,1,0:T(8,128)(2,1)S(1)}, bf16[1,128,256]{2,1,0:T(8,128)(2,1)S(1)}, u32[]{:S(2)}, u32[]{:S(2)}) %collective-permute-start.7) | collective-permute-done | bytes 65568 | tf_op jit(solution)/shard_map/ppermute | solution.py:15
  143.9 2.5 collective-permute-start.8
  146.4 1.6 collective-permute-start.9
  148.0 3.1 collective-permute-done.9
  151.9 1.2 pad.4
  153.1 2.3 reshape.39
  156.7 2.8 select_convert_fusion
  159.8 1.3 copy.59
  161.1 255.9 %all-reduce.3.cloned.1.call-done = (f32[589824]{0:T(1024)}, f32[1179648]{0:T(1024)}) async-done(((f32[589824]{0:T(1024)}, f32[1179648]{0:T(1024)}), (f32[589824]{0:T(1024)}, f32[1179648]{0:T(1024)})) %all-reduce.3.cloned.1.call-update) | async-done | bytes 7077904 | tf_op jit(solution)/shard_map/psum | solution.py:87
  417.1 3.6 multiply_reduce_fusion
  421.3 2.5 multiply_convert_fusion
  423.9 2.7 reshape.22
  426.6 2.9 multiply_reduce_fusion.1
  430.2 1.9 multiply_convert_fusion.1
  432.1 1.2 reshape.20
  (108 shorter events, 17.3 us)
Async XLA Ops:
  7.2 1.8 copy-start
  7.2 1.8 copy-start.27
  7.2 409.9 %all-reduce.3.cloned.1.call-start = ((), (), s32[]{:S(2)}) async-start(), calls=%async_computation | async-start | bytes 14155776 | tf_op jit(solution)/shard_map/psum | solution.py:87
  17.4 4.7 %copy-start.9 = (bf16[16,128,256]{2,1,0:T(8,128)(2,1)S(1)}, bf16[16,128,256]{2,1,0:T(8,128)(2,1)}, u32[]{:S(2)}) copy-start(bf16[16,128,256]{2,1,0:T(8,128)(2,1)} %param.4) | copy-start | bytes 3145732
  19.3 1.4 copy-start.4
  20.8 9.8 %collective-permute-start = (f32[17,1,256]{2,1,0:T(1,128)S(1)}, f32[17,1,256]{2,1,0:T(1,128)S(1)}, u32[]{:S(2)}, u32[]{:S(2)}) collective-permute-start(f32[17,1,256]{2,1,0:T(1,128)S(1)} %slice.157), channel_id=1, source_target_pairs={{1,0},{2,1},{3,2},{4,3},{5,4},{6,5},{7,6},{9,8},{10,9},{11,10},{12... | collective-permute-start | bytes 52232 | tf_op jit(solution)/shard_map/ppermute | solution.py:23
  22.8 10.2 %collective-permute-start.2 = (bf16[1,128,256]{1,2,0:T(8,128)(2,1)S(1)}, bf16[1,128,256]{1,2,0:T(8,128)(2,1)S(1)}, u32[]{:S(2)}, u32[]{:S(2)}) collective-permute-start(bf16[1,128,256]{1,2,0:T(8,128)(2,1)S(1)} %get-tuple-element.21), channel_id=1, source_target_pairs={{0,8},{8,16},{16,24},{24,32},{32,40},{40,48},{48,56},{56,64},{64,7... | collective-permute-start | bytes 196616 | tf_op jit(solution)/shard_map/ppermute | solution.py:14
  26.2 6.8 %collective-permute-start.3 = (bf16[1,128,256]{1,2,0:T(8,128)(2,1)S(1)}, bf16[1,128,256]{1,2,0:T(8,128)(2,1)S(1)}, u32[]{:S(2)}, u32[]{:S(2)}) collective-permute-start(bf16[1,128,256]{1,2,0:T(8,128)(2,1)S(1)} %get-tuple-element.22), channel_id=1, source_target_pairs={{8,0},{16,8},{24,16},{32,24},{40,32},{48,40},{56,48},{64,56},{72,6... | collective-permute-start | bytes 196616 | tf_op jit(solution)/shard_map/ppermute | solution.py:15
  36.8 8.1 %collective-permute-start.4 = (bf16[18,1,256]{2,0,1:T(8,128)(2,1)S(1)}, bf16[18,1,256]{2,0,1:T(8,128)(2,1)S(1)}, u32[]{:S(2)}, u32[]{:S(2)}) collective-permute-start(bf16[18,1,256]{2,0,1:T(8,128)(2,1)S(1)} %copy.41), channel_id=1, source_target_pairs={{0,1},{1,2},{2,3},{3,4},{4,5},{5,6},{6,7},{8,9},{9,10},{10,11},{11... | collective-permute-start | bytes 27656 | tf_op jit(solution)/shard_map/ppermute | solution.py:14
  41.1 5.4 %collective-permute-start.5 = (bf16[18,1,256]{2,0,1:T(8,128)(2,1)S(1)}, bf16[18,1,256]{2,0,1:T(8,128)(2,1)S(1)}, u32[]{:S(2)}, u32[]{:S(2)}) collective-permute-start(bf16[18,1,256]{2,0,1:T(8,128)(2,1)S(1)} %copy.42), channel_id=1, source_target_pairs={{1,0},{2,1},{3,2},{4,3},{5,4},{6,5},{7,6},{9,8},{10,9},{11,10},{12... | collective-permute-start | bytes 27656 | tf_op jit(solution)/shard_map/ppermute | solution.py:15
  43.1 28.3 %collective-permute-start.1 = (bf16[1,128,256]{2,1,0:T(8,128)(2,1)}, bf16[1,128,256]{2,1,0:T(8,128)(2,1)S(1)}, u32[]{:S(2)}, u32[]{:S(2)}) collective-permute-start(bf16[1,128,256]{2,1,0:T(8,128)(2,1)} %fusion.41), channel_id=1, source_target_pairs={{8,0},{16,8},{24,16},{32,24},{40,32},{48,40},{56,48},{64,56},{72,6... | collective-permute-start | bytes 196616 | tf_op jit(solution)/shard_map/ppermute | solution.py:23
  61.9 1.9 copy-start.24
  61.9 1.9 copy-start.26
  63.8 3.0 copy-start.2
  63.8 3.0 copy-start.3
  71.3 1.5 copy-start.5
  85.5 2.0 copy-start.8
  85.5 2.7 copy-start.7
  88.2 1.2 copy-start.10
  90.0 5.5 %copy-start.14 = (bf16[8,64,512]{2,1,0:T(8,128)(2,1)S(1)}, bf16[8,64,512]{2,1,0:T(8,128)(2,1)}, u32[]{:S(2)}) copy-start(bf16[8,64,512]{2,1,0:T(8,128)(2,1)} %param.7) | copy-start | bytes 1572868
  90.0 5.5 %copy-start.21 = (bf16[8,64,256]{2,1,0:T(8,128)(2,1)S(1)}, bf16[8,64,256]{2,1,0:T(8,128)(2,1)}, u32[]{:S(2)}) copy-start(bf16[8,64,256]{2,1,0:T(8,128)(2,1)} %slice.143) | copy-start | bytes 786436
  90.4 6.2 %copy-start.20 = (bf16[8,64,256]{2,1,0:T(8,128)(2,1)S(1)}, bf16[8,64,256]{2,1,0:T(8,128)(2,1)}, u32[]{:S(2)}) copy-start(bf16[8,64,256]{2,1,0:T(8,128)(2,1)} %slice.142) | copy-start | bytes 786436
  91.0 6.8 %copy-start.19 = (bf16[8,64,256]{2,1,0:T(8,128)(2,1)S(1)}, bf16[8,64,256]{2,1,0:T(8,128)(2,1)}, u32[]{:S(2)}) copy-start(bf16[8,64,256]{2,1,0:T(8,128)(2,1)} %slice.146) | copy-start | bytes 786436
  91.0 7.9 %copy-start.18 = (bf16[8,64,256]{2,1,0:T(8,128)(2,1)S(1)}, bf16[8,64,256]{2,1,0:T(8,128)(2,1)}, u32[]{:S(2)}) copy-start(bf16[8,64,256]{2,1,0:T(8,128)(2,1)} %slice.145) | copy-start | bytes 786436
  91.0 12.9 %collective-permute-start.10 = (bf16[16,1,256]{2,1,0:T(2,128)(2,1)S(1)}, bf16[16,1,256]{2,1,0:T(2,128)(2,1)S(1)}, u32[]{:S(2)}, u32[]{:S(2)}) collective-permute-start(bf16[16,1,256]{2,1,0:T(2,128)(2,1)S(1)} %slice.178), channel_id=1, source_target_pairs={{0,1},{1,2},{2,3},{3,4},{4,5},{5,6},{6,7},{8,9},{9,10},{10,11},{11... | collective-permute-start | bytes 24584 | tf_op jit(solution)/shard_map/ppermute | solution.py:23
  103.9 9.7 %copy-start.22 = (bf16[16,1,256]{2,1,0:T(2,128)(2,1)}, bf16[16,1,256]{2,1,0:T(2,128)(2,1)S(1)}, u32[]{:S(2)}) copy-start(bf16[16,1,256]{2,1,0:T(2,128)(2,1)S(1)} %collective-permute-done.10) | copy-start | bytes 24580
  107.5 6.1 %copy-start.15 = (bf16[8,64,512]{2,1,0:T(8,128)(2,1)S(1)}, bf16[8,64,512]{2,1,0:T(8,128)(2,1)}, u32[]{:S(2)}) copy-start(bf16[8,64,512]{2,1,0:T(8,128)(2,1)} %param.7) | copy-start | bytes 1572868
  107.5 6.4 %copy-start.16 = (f32[1,256,512]{2,1,0:T(8,128)S(1)}, f32[1,256,512]{2,1,0:T(8,128)}, u32[]{:S(2)}) copy-start(f32[1,256,512]{2,1,0:T(8,128)} %convolution_bitcast_fusion) | copy-start | bytes 1572868
  107.5 6.4 %copy-start.17 = (f32[1,256,512]{2,1,0:T(8,128)S(1)}, f32[1,256,512]{2,1,0:T(8,128)}, u32[]{:S(2)}) copy-start(f32[1,256,512]{2,1,0:T(8,128)} %convolution_bitcast_fusion.1) | copy-start | bytes 1572868
  107.5 7.7 %collective-permute-start.11 = (bf16[1,129,256]{2,1,0:T(8,128)(2,1)S(1)}, bf16[1,129,256]{2,1,0:T(8,128)(2,1)S(1)}, u32[]{:S(2)}, u32[]{:S(2)}) collective-permute-start(bf16[1,129,256]{2,1,0:T(8,128)(2,1)S(1)} %fusion.42), channel_id=1, source_target_pairs={{0,8},{8,16},{16,24},{24,32},{32,40},{40,48},{48,56},{56,64},{64,7... | collective-permute-start | bytes 198152 | tf_op jit(solution)/shard_map/ppermute | solution.py:23
  113.9 1.3 copy-start.23
  121.5 4.4 copy-start.11
  121.5 4.4 copy-start.12
  121.5 4.4 copy-start.13
  125.9 1.4 copy-start.6
  131.3 6.7 %collective-permute-start.6 = (bf16[1,128,256]{2,1,0:T(8,128)(2,1)S(1)}, bf16[1,128,256]{2,1,0:T(8,128)(2,1)S(1)}, u32[]{:S(2)}, u32[]{:S(2)}) collective-permute-start(bf16[1,128,256]{2,1,0:T(8,128)(2,1)S(1)} %get-tuple-element.19), channel_id=1, source_target_pairs={{0,8},{8,16},{16,24},{24,32},{32,40},{40,48},{48,56},{56,64},{64,7... | collective-permute-start | bytes 196616 | tf_op jit(solution)/shard_map/ppermute | solution.py:14
  135.9 8.0 %collective-permute-start.7 = (bf16[1,128,256]{2,1,0:T(8,128)(2,1)S(1)}, bf16[1,128,256]{2,1,0:T(8,128)(2,1)S(1)}, u32[]{:S(2)}, u32[]{:S(2)}) collective-permute-start(bf16[1,128,256]{2,1,0:T(8,128)(2,1)S(1)} %get-tuple-element.20), channel_id=1, source_target_pairs={{8,0},{16,8},{24,16},{32,24},{40,32},{48,40},{56,48},{64,56},{72,6... | collective-permute-start | bytes 196616 | tf_op jit(solution)/shard_map/ppermute | solution.py:15
  143.9 4.1 collective-permute-start.8
  146.4 4.7 %collective-permute-start.9 = (bf16[18,1,256]{2,1,0:T(2,128)(2,1)S(1)}, bf16[18,1,256]{2,1,0:T(2,128)(2,1)S(1)}, u32[]{:S(2)}, u32[]{:S(2)}) collective-permute-start(bf16[18,1,256]{2,1,0:T(2,128)(2,1)S(1)} %get-tuple-element.16), channel_id=1, source_target_pairs={{1,0},{2,1},{3,2},{4,3},{5,4},{6,5},{7,6},{9,8},{10,9},{11,10},{12... | collective-permute-start | bytes 27656 | tf_op jit(solution)/shard_map/ppermute | solution.py:15
  155.4 1.3 copy-start.25
  430.1 3.2 copy-start.1
Sparse Core Ops, SparseCore 0:
  131.4 285.6 all-reduce.2
where the time goes:
time: 441 us; the launch traced here: 440 us
  waiting for transfers between devices  265 us (60%)
  local copies, waits for them, and re-layouts  74.5 us (17%)
  starting transfers between devices  31.7 us (7%)
  other arithmetic  28 us (6%)
  matrix products  24.6 us (6%)
  between operations  16.2 us (4%)
    psum x1, waiting for transfers between devices, on_device(): total_one, total_two = lax.psum((flat_one, flat_two), ('row', 'col'))  256 us
    slice x9, local copies, waits for them, and re-layouts, on_device(): act_pad[row_off:row_off + rows_here - 1:2, col_off:col_off + cols_here -...  19.8 us
    unnamed x62, local copies, waits for them, and re-layouts  18.9 us
    conv_general_dilated x12, local copies, waits for them, and re-layouts, conv_local(): lax.conv_general_dilated(source[None], kernel, (1, 1), padding, lhs_dilat...  15.6 us
    ppermute x4, starting transfers between devices, padded(): before = lax.ppermute(last, axis, up)  13 us
    dot_general x9, matrix products, on_device(): jnp.einsum('ijc,ije->ce', patch, cotangent, preferred_element_type=jnp.fl...  11.4 us
    ppermute x4, starting transfers between devices, passed_along(): return lax.ppermute(shard, axis, pairs)  11.4 us
    ppermute x4, waiting for transfers between devices, padded(): after = lax.ppermute(initial, axis, down)  9.07 us
  transfers between devices with their start and end apart: 13, of which 4 were waited for; matrix products, arithmetic and copies ran while one was open for 12% of the time, Pallas kernels for 0%

commit v1 on v0

--- a/solution.py
+++ b/solution.py
@@ -84,7 +84,7 @@
     )
     flat_one = grad_one.reshape(-1)
     flat_two = grad_two.reshape(-1)
-    total_one, total_two = lax.psum((flat_one, flat_two), ("row", "col"))
+    total_one, total_two = lax.psum(lax.psum((flat_one, flat_two), "col"), "row")
     update_one = (total_one * lax.rsqrt(jnp.mean(total_one * total_one) + 1e-06)).astype(
         jnp.bfloat16
     )

time: 441 us -> 461 us (1.045)
  waiting for transfers between devices: 265 us -> 286 us
    psum x1 -> x2, waiting for transfers between devices: 256 us -> 281 us  [the longest x1 174 us: on_device(): lax.psum(lax.psum((flat_one, flat_two), 'col'), 'row')]
  transfers between devices with their start and end apart: 13 -> 14, of which waited for: 4 -> 5; matrix products, arithmetic and copies ran while one was open for 12% -> 12% of each run, Pallas kernels for 0% -> 0%
where the time goes in v1:
time: 461 us; the launch traced here: 459 us
  waiting for transfers between devices  286 us (62%)
  local copies, waits for them, and re-layouts  74.5 us (16%)
  starting transfers between devices  29.8 us (6%)
  other arithmetic  28.1 us (6%)
  matrix products  24.6 us (5%)
  between operations  16.2 us (4%)
    psum x1, waiting for transfers between devices, on_device(): lax.psum(lax.psum((flat_one, flat_two), 'col'), 'row')  174 us
    psum x1, waiting for transfers between devices, on_device(): lax.psum((flat_one, flat_two), 'col')  107 us
    slice x9, local copies, waits for them, and re-layouts, on_device(): act_pad[row_off:row_off + rows_here - 1:2, col_off:col_off + cols_here -...  19.8 us
    unnamed x62, local copies, waits for them, and re-layouts  19 us
    conv_general_dilated x12, local copies, waits for them, and re-layouts, conv_local(): lax.conv_general_dilated(source[None], kernel, (1, 1), padding, lhs_dilat...  15.6 us
    dot_general x9, matrix products, on_device(): jnp.einsum('ijc,ije->ce', patch, cotangent, preferred_element_type=jnp.fl...  11.4 us
    ppermute x4, starting transfers between devices, passed_along(): return lax.ppermute(shard, axis, pairs)  11.4 us
    ppermute x4, starting transfers between devices, padded(): before = lax.ppermute(last, axis, up)  10.5 us
  transfers between devices with their start and end apart: 14, of which 5 were waited for; matrix products, arithmetic and copies ran while one was open for 12% of the time, Pallas kernels for 0%

profile of v1, /device:TPU:2, one launch (start us, length us, event | category | flops | bytes accessed | tf_op | source)
XLA Modules:
  0.0 459.2 jit_solution(3829064986734693746)
XLA Ops:
  7.2 1.5 copy.73
  9.0 1.7 convolution_select_fusion
  10.7 2.6 copy.37
  13.3 4.1 reshape.29
  17.4 1.9 slice_bitcast_fusion
  19.4 1.4 copy-done.4
  20.8 1.3 collective-permute-start
  22.8 3.4 collective-permute-start.2
  26.2 2.4 collective-permute-start.3
  28.6 1.9 slice.155
  31.5 1.5 fusion.4
  33.2 1.9 fusion.54
  35.1 1.8 copy.41
  36.9 2.5 collective-permute-start.4
  39.3 1.8 copy.42
  41.1 1.3 collective-permute-start.5
  43.1 1.9 collective-permute-start.1
  45.0 1.5 copy.43
  46.5 1.5 copy.44
  48.0 4.4 maximum_bitcast_fusion
  52.3 3.9 copy.64
  56.2 2.4 pad.2.clone
  58.6 3.2 reshape.32
  61.9 1.9 copy.47
  63.9 3.0 convolution_select_fusion.1
  66.9 3.6 maximum_maximum_fusion
  71.5 1.5 copy-done.5
  73.0 1.8 multiply_convert_fusion.2
  74.8 2.7 slice.143
  77.5 2.7 slice.142
  80.1 2.7 slice.146
  82.9 2.7 slice.145
  85.6 1.8 convolution_bitcast_fusion.15
  91.1 4.4 collective-permute-start.10
  96.7 1.1 convolution_bitcast_fusion.4
  101.3 2.6 copy.65
  104.4 2.7 slice.141
  107.6 3.8 collective-permute-start.11
  111.4 2.3 convolution_bitcast_fusion.5
  114.0 1.3 maximum_bitcast_fusion.3
  115.7 2.7 slice.140
  118.5 2.7 slice.139
  121.6 1.5 convolution_bitcast_fusion.6
  123.2 1.4 convolution_bitcast_fusion.7
  124.6 1.4 convolution_bitcast_fusion.8
  127.9 3.4 copy.66
  131.4 106.7 %all-reduce.7.cloned.1.call-done = (f32[589824]{0:T(1024)}, f32[1179648]{0:T(1024)}) async-done(((f32[589824]{0:T(1024)}, f32[1179648]{0:T(1024)}), (f32[589824]{0:T(1024)}, f32[1179648]{0:T(1024)})) %all-reduce.7.cloned.1.call-update) | async-done | bytes 7077904 | tf_op jit(solution)/shard_map/psum | solution.py:87
  238.1 3.4 collective-permute-start.6
  241.5 2.5 collective-permute-start.7
  244.3 3.4 collective-permute-done.7
  247.7 1.3 collective-permute-start.8
  249.0 1.6 collective-permute-start.9
  250.5 1.7 collective-permute-done.9
  253.0 1.1 pad.4
  254.1 2.3 reshape.39
  257.7 2.8 select_convert_fusion
  260.8 1.3 copy.59
  262.1 174.0 %all-reduce.5.cloned.1.call-done = (f32[589824]{0:T(1024)}, f32[1179648]{0:T(1024)}) async-done(((f32[589824]{0:T(1024)}, f32[1179648]{0:T(1024)}), (f32[589824]{0:T(1024)}, f32[1179648]{0:T(1024)})) %all-reduce.5.cloned.1.call-update) | async-done | bytes 7077904 | tf_op jit(solution)/shard_map/psum | solution.py:87
  436.1 3.6 multiply_reduce_fusion
  440.4 2.5 multiply_convert_fusion
  442.9 2.7 reshape.22
  445.6 2.9 multiply_reduce_fusion.1
  449.2 1.9 multiply_convert_fusion.1
  451.1 1.2 reshape.20
  (111 shorter events, 18.6 us)
Async XLA Ops:
  7.2 1.8 copy-start
  7.2 1.8 copy-start.27
  7.2 230.9 %all-reduce.7.cloned.1.call-start = ((), (), s32[]{:S(2)}) async-start(), calls=%async_computation.1 | async-start | bytes 14155776 | tf_op jit(solution)/shard_map/psum | solution.py:87
  17.4 4.6 %copy-start.9 = (bf16[16,128,256]{2,1,0:T(8,128)(2,1)S(1)}, bf16[16,128,256]{2,1,0:T(8,128)(2,1)}, u32[]{:S(2)}) copy-start(bf16[16,128,256]{2,1,0:T(8,128)(2,1)} %param.4) | copy-start | bytes 3145732
  19.3 1.4 copy-start.4
  20.8 9.8 %collective-permute-start = (f32[17,1,256]{2,1,0:T(1,128)S(1)}, f32[17,1,256]{2,1,0:T(1,128)S(1)}, u32[]{:S(2)}, u32[]{:S(2)}) collective-permute-start(f32[17,1,256]{2,1,0:T(1,128)S(1)} %slice.157), channel_id=1, source_target_pairs={{1,0},{2,1},{3,2},{4,3},{5,4},{6,5},{7,6},{9,8},{10,9},{11,10},{12... | collective-permute-start | bytes 52232 | tf_op jit(solution)/shard_map/ppermute | solution.py:23
  22.8 10.2 %collective-permute-start.2 = (bf16[1,128,256]{1,2,0:T(8,128)(2,1)S(1)}, bf16[1,128,256]{1,2,0:T(8,128)(2,1)S(1)}, u32[]{:S(2)}, u32[]{:S(2)}) collective-permute-start(bf16[1,128,256]{1,2,0:T(8,128)(2,1)S(1)} %get-tuple-element.23), channel_id=1, source_target_pairs={{0,8},{8,16},{16,24},{24,32},{32,40},{40,48},{48,56},{56,64},{64,7... | collective-permute-start | bytes 196616 | tf_op jit(solution)/shard_map/ppermute | solution.py:14
  26.2 6.8 %collective-permute-start.3 = (bf16[1,128,256]{1,2,0:T(8,128)(2,1)S(1)}, bf16[1,128,256]{1,2,0:T(8,128)(2,1)S(1)}, u32[]{:S(2)}, u32[]{:S(2)}) collective-permute-start(bf16[1,128,256]{1,2,0:T(8,128)(2,1)S(1)} %get-tuple-element.24), channel_id=1, source_target_pairs={{8,0},{16,8},{24,16},{32,24},{40,32},{48,40},{56,48},{64,56},{72,6... | collective-permute-start | bytes 196616 | tf_op jit(solution)/shard_map/ppermute | solution.py:15
  36.9 8.1 %collective-permute-start.4 = (bf16[18,1,256]{2,0,1:T(8,128)(2,1)S(1)}, bf16[18,1,256]{2,0,1:T(8,128)(2,1)S(1)}, u32[]{:S(2)}, u32[]{:S(2)}) collective-permute-start(bf16[18,1,256]{2,0,1:T(8,128)(2,1)S(1)} %copy.41), channel_id=1, source_target_pairs={{0,1},{1,2},{2,3},{3,4},{4,5},{5,6},{6,7},{8,9},{9,10},{10,11},{11... | collective-permute-start | bytes 27656 | tf_op jit(solution)/shard_map/ppermute | solution.py:14
  41.1 5.4 %collective-permute-start.5 = (bf16[18,1,256]{2,0,1:T(8,128)(2,1)S(1)}, bf16[18,1,256]{2,0,1:T(8,128)(2,1)S(1)}, u32[]{:S(2)}, u32[]{:S(2)}) collective-permute-start(bf16[18,1,256]{2,0,1:T(8,128)(2,1)S(1)} %copy.42), channel_id=1, source_target_pairs={{1,0},{2,1},{3,2},{4,3},{5,4},{6,5},{7,6},{9,8},{10,9},{11,10},{12... | collective-permute-start | bytes 27656 | tf_op jit(solution)/shard_map/ppermute | solution.py:15
  43.1 28.4 %collective-permute-start.1 = (bf16[1,128,256]{2,1,0:T(8,128)(2,1)}, bf16[1,128,256]{2,1,0:T(8,128)(2,1)S(1)}, u32[]{:S(2)}, u32[]{:S(2)}) collective-permute-start(bf16[1,128,256]{2,1,0:T(8,128)(2,1)} %fusion.41), channel_id=1, source_target_pairs={{8,0},{16,8},{24,16},{32,24},{40,32},{48,40},{56,48},{64,56},{72,6... | collective-permute-start | bytes 196616 | tf_op jit(solution)/shard_map/ppermute | solution.py:23
  61.9 1.9 copy-start.24
  61.9 1.9 copy-start.26
  63.8 3.0 copy-start.2
  63.8 3.0 copy-start.3
  71.4 1.5 copy-start.5
  85.6 2.0 copy-start.8
  85.6 2.7 copy-start.7
  88.3 1.2 copy-start.10
  90.1 5.5 %copy-start.14 = (bf16[8,64,512]{2,1,0:T(8,128)(2,1)S(1)}, bf16[8,64,512]{2,1,0:T(8,128)(2,1)}, u32[]{:S(2)}) copy-start(bf16[8,64,512]{2,1,0:T(8,128)(2,1)} %param.7) | copy-start | bytes 1572868
  90.1 5.5 %copy-start.21 = (bf16[8,64,256]{2,1,0:T(8,128)(2,1)S(1)}, bf16[8,64,256]{2,1,0:T(8,128)(2,1)}, u32[]{:S(2)}) copy-start(bf16[8,64,256]{2,1,0:T(8,128)(2,1)} %slice.143) | copy-start | bytes 786436
  90.5 6.1 %copy-start.20 = (bf16[8,64,256]{2,1,0:T(8,128)(2,1)S(1)}, bf16[8,64,256]{2,1,0:T(8,128)(2,1)}, u32[]{:S(2)}) copy-start(bf16[8,64,256]{2,1,0:T(8,128)(2,1)} %slice.142) | copy-start | bytes 786436
  91.1 6.7 %copy-start.19 = (bf16[8,64,256]{2,1,0:T(8,128)(2,1)S(1)}, bf16[8,64,256]{2,1,0:T(8,128)(2,1)}, u32[]{:S(2)}) copy-start(bf16[8,64,256]{2,1,0:T(8,128)(2,1)} %slice.146) | copy-start | bytes 786436
  91.1 7.8 %copy-start.18 = (bf16[8,64,256]{2,1,0:T(8,128)(2,1)S(1)}, bf16[8,64,256]{2,1,0:T(8,128)(2,1)}, u32[]{:S(2)}) copy-start(bf16[8,64,256]{2,1,0:T(8,128)(2,1)} %slice.145) | copy-start | bytes 786436
  91.1 12.8 %collective-permute-start.10 = (bf16[16,1,256]{2,1,0:T(2,128)(2,1)S(1)}, bf16[16,1,256]{2,1,0:T(2,128)(2,1)S(1)}, u32[]{:S(2)}, u32[]{:S(2)}) collective-permute-start(bf16[16,1,256]{2,1,0:T(2,128)(2,1)S(1)} %slice.178), channel_id=1, source_target_pairs={{0,1},{1,2},{2,3},{3,4},{4,5},{5,6},{6,7},{8,9},{9,10},{10,11},{11... | collective-permute-start | bytes 24584 | tf_op jit(solution)/shard_map/ppermute | solution.py:23
  103.9 9.7 %copy-start.22 = (bf16[16,1,256]{2,1,0:T(2,128)(2,1)}, bf16[16,1,256]{2,1,0:T(2,128)(2,1)S(1)}, u32[]{:S(2)}) copy-start(bf16[16,1,256]{2,1,0:T(2,128)(2,1)S(1)} %collective-permute-done.10) | copy-start | bytes 24580
  107.5 6.1 %copy-start.15 = (bf16[8,64,512]{2,1,0:T(8,128)(2,1)S(1)}, bf16[8,64,512]{2,1,0:T(8,128)(2,1)}, u32[]{:S(2)}) copy-start(bf16[8,64,512]{2,1,0:T(8,128)(2,1)} %param.7) | copy-start | bytes 1572868
  107.5 6.4 %copy-start.16 = (f32[1,256,512]{2,1,0:T(8,128)S(1)}, f32[1,256,512]{2,1,0:T(8,128)}, u32[]{:S(2)}) copy-start(f32[1,256,512]{2,1,0:T(8,128)} %convolution_bitcast_fusion) | copy-start | bytes 1572868
  107.6 6.4 %copy-start.17 = (f32[1,256,512]{2,1,0:T(8,128)S(1)}, f32[1,256,512]{2,1,0:T(8,128)}, u32[]{:S(2)}) copy-start(f32[1,256,512]{2,1,0:T(8,128)} %convolution_bitcast_fusion.1) | copy-start | bytes 1572868
  107.6 7.7 %collective-permute-start.11 = (bf16[1,129,256]{2,1,0:T(8,128)(2,1)S(1)}, bf16[1,129,256]{2,1,0:T(8,128)(2,1)S(1)}, u32[]{:S(2)}, u32[]{:S(2)}) collective-permute-start(bf16[1,129,256]{2,1,0:T(8,128)(2,1)S(1)} %fusion.42), channel_id=1, source_target_pairs={{0,8},{8,16},{16,24},{24,32},{32,40},{40,48},{48,56},{56,64},{64,7... | collective-permute-start | bytes 198152 | tf_op jit(solution)/shard_map/ppermute | solution.py:23
  114.0 1.3 copy-start.23
  121.6 4.4 copy-start.11
  121.6 4.4 copy-start.12
  121.6 4.4 copy-start.13
  126.0 1.4 copy-start.6
  131.3 304.7 %all-reduce.5.cloned.1.call-start = ((), (), s32[]{:S(2)}) async-start(), calls=%async_computation | async-start | bytes 14155776 | tf_op jit(solution)/shard_map/psum | solution.py:87
  238.1 6.2 %collective-permute-start.6 = (bf16[1,128,256]{2,1,0:T(8,128)(2,1)S(1)}, bf16[1,128,256]{2,1,0:T(8,128)(2,1)S(1)}, u32[]{:S(2)}, u32[]{:S(2)}) collective-permute-start(bf16[1,128,256]{2,1,0:T(8,128)(2,1)S(1)} %get-tuple-element.21), channel_id=1, source_target_pairs={{0,8},{8,16},{16,24},{24,32},{32,40},{40,48},{48,56},{56,64},{64,7... | collective-permute-start | bytes 196616 | tf_op jit(solution)/shard_map/ppermute | solution.py:14
  241.5 6.2 %collective-permute-start.7 = (bf16[1,128,256]{2,1,0:T(8,128)(2,1)S(1)}, bf16[1,128,256]{2,1,0:T(8,128)(2,1)S(1)}, u32[]{:S(2)}, u32[]{:S(2)}) collective-permute-start(bf16[1,128,256]{2,1,0:T(8,128)(2,1)S(1)} %get-tuple-element.22), channel_id=1, source_target_pairs={{8,0},{16,8},{24,16},{32,24},{40,32},{48,40},{56,48},{64,56},{72,6... | collective-permute-start | bytes 196616 | tf_op jit(solution)/shard_map/ppermute | solution.py:15
  247.7 2.9 collective-permute-start.8
  249.0 3.2 collective-permute-start.9
  256.4 1.3 copy-start.25
  449.1 3.2 copy-start.1
Sparse Core Ops, SparseCore 0:
  131.5 106.5 all-reduce.6
  241.8 194.2 all-reduce.4
